TPU v7x, 512 devices: a whole 4x8x8 slice. The times are simulated.
512 devices in a mesh: seq: 64 (over y, x, core), head: 8 (over z).
Axes of the slice: x: 4, y: 8, z: 8, core: 2. Of those that a mesh axis runs over, the one named last changes fastest.
Arguments:
- stacked_keys: bfloat16 [196608, 4096], P('seq', 'head'), parts along dimension 1, may hold values from -6 to 6
- sketch: bfloat16 [512, 160], replicated, may hold values from -0.25 to 0.25
Outputs:
- basis: bfloat16 [196608, 1280], P('seq', 'head'), parts along dimension 1
- coefficients: float32 [1280, 512], P('head'), parts along dimension 0
There are 8 independent parts, one for each index of `head`. A program takes and returns all parts, laid end to end along the dimension named above; an argument that names none is the same for every part. Nothing has to cross between parts.
All inputs are finite; a program needn't handle non-finite values.
Results may differ from a plain program's by a relative error of at most 0.001.
Values sent between devices are 32-bit elements; how exact they have to be, the bound alone decides.
No kernel may reach another device: no remote copies, remote signals or barrier semaphores. Data moves between devices by JAX's collectives and lax.ppermute only.
A program may use at most 64 MiB of HBM per device.

v0:
```python
import jax
import jax.numpy as jnp
from jax import lax
from jax.sharding import PartitionSpec as P


def invert_lower(gram):
    lower = jnp.linalg.cholesky(gram)
    eye_mat = jnp.eye(gram.shape[0], dtype=gram.dtype)
    return lax.linalg.triangular_solve(lower, eye_mat, left_side=True, lower=True)


def split_product(left, keys):
    high_part = left.astype(jnp.bfloat16)
    low_part = (left - high_part.astype(jnp.float32)).astype(jnp.bfloat16)
    dims = (((0,), (0,)), ((), ()))
    first = lax.dot_general(high_part, keys, dims, preferred_element_type=jnp.float32)
    second = lax.dot_general(low_part, keys, dims, preferred_element_type=jnp.float32)
    return first + second


def body(stacked_keys, sketch):
    sampled = jnp.dot(stacked_keys, sketch, preferred_element_type=jnp.float32)
    total_rows = stacked_keys.shape[0] * lax.axis_size("seq")
    local_gram = lax.dot_general(
        sampled, sampled, (((0,), (0,)), ((), ())), precision=lax.Precision.HIGHEST
    )
    gram = lax.psum(local_gram, "seq")
    inverse = invert_lower(gram)
    orthonormal = jnp.dot(sampled, inverse.T, precision=lax.Precision.HIGHEST)
    local_coef = split_product(orthonormal, stacked_keys)
    coefficients = lax.psum(local_coef, "seq")
    basis = (orthonormal * jnp.sqrt(jnp.float32(total_rows))).astype(jnp.bfloat16)
    return (basis, coefficients)


def solution(mesh):
    return jax.shard_map(
        body,
        mesh=mesh,
        in_specs=(P("seq", "head"), P()),
        out_specs=(P("seq", "head"), P("head", None)),
        check_vma=False,
    )
```

profile of v0, /device:TPU:1, one launch (start us, length us, event | category | flops | bytes accessed | tf_op | source)
XLA Modules:
  0.0 465.6 jit_solution(6867001046641380688)
XLA Ops:
  7.2 0.0 copy-start
  7.2 0.0 all-reduce.6.cloned.1.call-start
  7.2 1.8 copy-done
  9.1 2.1 fusion.17
  11.1 0.0 copy-start.1
  11.2 1.3 copy-done.1
  12.4 2.4 fusion.18
  14.8 0.0 all-reduce.6.cloned.1.call-update
  14.8 0.0 all-reduce.8.cloned.1.call-start
  14.9 0.6 iota_compare_fusion
  15.6 191.5 %all-reduce.6.cloned.1.call-done = f32[160,160]{0,1:T(8,128)} async-done(((f32[160,160]{0,1:T(8,128)}), f32[160,160]{0,1:T(8,128)}) %all-reduce.6.cloned.1.call-update) | async-done | bytes 102416 | tf_op jit(solution)/shard_map/psum | solution.py:28
  207.1 1.0 copy.5
  208.1 0.9 fusion.7
  209.1 11.7 %cholesky.51 = f32[128,128]{1,0:T(8,128)S(1)} custom-call(f32[128,128]{1,0:T(8,128)S(1)} %cholesky.124), custom_call_target="Cholesky" | custom-call | tf_op jit(solution)/shard_map/jit(cholesky)/cholesky | solution.py:8
  220.8 0.0 copy-start.2
  220.8 0.7 compare_reduce_fusion.1
  221.5 0.0 copy-done.2
  221.5 10.4 %custom-call.14 = f32[1,128,128]{1,2,0:T(8,128)} custom-call(f32[1,128,128]{2,1,0:T(8,128)S(1)} %get-tuple-element.23), custom_call_target="InvertDiagBlocksLowerTriangular" | custom-call | tf_op jit(solution)/shard_map/jit(cholesky)/cholesky | solution.py:8
  231.9 0.9 cholesky.119
  232.8 1.0 constant_dynamic-update-slice_fusion.1
  233.8 0.2 convolution_subtract_fusion.1
  233.9 2.9 cholesky.110
  236.9 0.6 compare_reduce_fusion
  238.9 0.1 fusion.10
  239.0 0.7 pad_maximum_fusion
  239.6 20.5 %custom-call.15 = f32[2,128,128]{1,2,0:T(8,128)S(1)} custom-call(f32[2,128,128]{2,1,0:T(8,128)} %pad_maximum_fusion), custom_call_target="InvertDiagBlocksLowerTriangular" | custom-call | tf_op jit(solution)/shard_map/triangular_solve | solution.py:10
  260.1 1.0 fusion.8
  261.1 1.0 convolution_subtract_fusion
  262.1 0.3 fusion.14
  262.4 4.5 multiply_convert_fusion
  266.9 0.7 fusion.1
  267.7 1.5 convolution_add_fusion
  269.1 0.0 all-reduce.8.cloned.1.call-update
  269.2 187.9 %all-reduce.8.cloned.1.call-done = f32[160,512]{1,0:T(8,128)} async-done(((f32[160,512]{1,0:T(8,128)}), f32[160,512]{1,0:T(8,128)}) %all-reduce.8.cloned.1.call-update) | async-done | bytes 327696 | tf_op jit(solution)/shard_map/psum | solution.py:32
  457.1 1.7 copy.12
  (7 shorter events, 0.1 us)
Async XLA Ops:
  7.2 1.9 copy-start
  7.2 199.9 %all-reduce.6.cloned.1.call-start = ((), (), s32[]{:S(2)}) async-start(), calls=%async_computation | async-start | bytes 327680 | tf_op jit(solution)/shard_map/psum | solution.py:28
  11.1 1.3 copy-start.1
  14.8 442.2 %all-reduce.8.cloned.1.call-start = ((), (), s32[]{:S(2)}) async-start(), calls=%async_computation.1 | async-start | bytes 655360 | tf_op jit(solution)/shard_map/psum | solution.py:32
  220.8 0.7 copy-start.2
Sparse Core Ops, SparseCore 0:
  15.0 192.0 all-reduce.5
  269.3 187.7 all-reduce.7
where the time goes:
time: 466 us
  waiting for transfers between devices  379 us (81%)
  other arithmetic  49.3 us (11%)
  between operations  15.5 us (3%)
  matrix products  14.6 us (3%)
  local copies, waits for them, and re-layouts  6.72 us (1%)
    psum x1, waiting for transfers between devices, body(): gram = lax.psum(local_gram, 'seq')  191 us
    psum x1, waiting for transfers between devices, body(): coefficients = lax.psum(local_coef, 'seq')  188 us
    another operation x7, other arithmetic, invert_lower(): lower = jnp.linalg.cholesky(gram)  26.4 us
    another operation x6, other arithmetic, invert_lower(): lax.linalg.triangular_solve(lower, eye_mat, left_side=True, lower=True)  21.3 us
  transfers between devices with their start and end apart: 2, of which 2 were waited for; matrix products, arithmetic and copies ran while one was open for 0% of the time, Pallas kernels for 0%

commit v1 on v0

v1 whole, which is shorter than its diff:
```python
import functools

import jax
import jax.numpy as jnp
from jax import lax
from jax.experimental import pallas as pl
from jax.experimental.pallas import tpu as pltpu
from jax.sharding import Mesh, PartitionSpec as P

INNER = 16
ROWS_OUT, COLS_OUT = 40, 128
F32, BF16 = jnp.float32, jnp.bfloat16
MIB = 1 << 20


def dot(a, b, ca, cb):
    return lax.dot_general(a, b, (((ca,), (cb,)), ((), ())), preferred_element_type=F32)


def split3(x):
    a = x.astype(BF16)
    rest = x - a.astype(F32)
    b = rest.astype(BF16)
    return a, b, (rest - b.astype(F32)).astype(BF16)


def moments_kernel(k_ref, s_ref, m_ref, acc):
    step = pl.program_id(0)
    keys = k_ref[...]
    part = dot(keys, keys, 0, 0)

    @pl.when(step == 0)
    def _():
        acc[...] = part

    @pl.when(step > 0)
    def _():
        acc[...] += part

    @pl.when(step == pl.num_programs(0) - 1)
    def _():
        sketch = s_ref[...]
        total = jnp.zeros((sketch.shape[1], acc.shape[1]), F32)
        for piece in reversed(split3(acc[...])):
            total += dot(sketch, piece, 0, 0)
        put_chunks(m_ref, total)


def put_chunks(ref, m):
    wide = m.shape[1] // COLS_OUT
    for i in range(ref.shape[0]):
        r, c = i // wide * ROWS_OUT, i % wide * COLS_OUT
        ref[i] = m[r : r + ROWS_OUT, c : c + COLS_OUT]


def moments(keys, sketch, block=1024):
    tokens, cols = keys.shape
    rank = sketch.shape[1]
    chunks = (rank // ROWS_OUT) * (cols // COLS_OUT)
    return pl.pallas_call(
        moments_kernel,
        grid=(tokens // block,),
        out_shape=jax.ShapeDtypeStruct((chunks, ROWS_OUT, COLS_OUT), F32),
        in_specs=[
            pl.BlockSpec((block, cols), lambda i: (i, 0)),
            pl.BlockSpec((cols, rank), lambda i: (0, 0)),
        ],
        out_specs=pl.BlockSpec((chunks, ROWS_OUT, COLS_OUT), lambda i: (0, 0, 0)),
        scratch_shapes=[pltpu.VMEM((cols, cols), F32)],
        compiler_params=pltpu.CompilerParams(vmem_limit_bytes=24 * MIB),
        name="moments",
    )(keys, sketch)


def lanes_of(tile, j):
    return jnp.broadcast_to(tile[:, j : j + 1], (8, 128))


def row_of(tile, s):
    return jnp.broadcast_to(tile[s : s + 1, :], (8, 128))


def invert_factor(t):
    n, wide = len(t), len(t[0])
    sub = lax.broadcasted_iota(jnp.int32, (8, 128), 0)
    lane = lax.broadcasted_iota(jnp.int32, (8, 128), 1)
    for b in range(n):
        at, off = b // 16, 8 * (b % 16)
        cols = [lanes_of(t[b][at], off + s) for s in range(8)]
        solved, factor = list(t[b]), list(t[b])
        for s in range(8):
            here = sub == s
            pivot = row_of(cols[s], s)
            inv, root = 1.0 / pivot, lax.rsqrt(pivot)
            for h in range(wide):
                row, old = row_of(solved[h], s), solved[h]
                if h == at:
                    row = jnp.where(lane == off + s, 1.0, row)
                    old = jnp.where(lane == off + s, 0.0, old)
                factor[h] = jnp.where(here, row * root, factor[h])
                row = row * inv
                solved[h] = jnp.where(here, row, old - cols[s] * row)
            for k in range(s + 1, 8):
                val = row_of(cols[k], s) * inv
                cols[k] = jnp.where(here, val, cols[k] - cols[s] * val)
        in_block = (lane >= off) & (lane < off + 8)
        for i in range(b + 1, n):
            left = [lanes_of(t[i][at], off + s) for s in range(8)]
            for h in range(wide):
                x = t[i][h]
                if h == at:
                    x = jnp.where(in_block, 0.0, x)
                parts = [left[s] * row_of(solved[h], s) for s in range(8)]
                while len(parts) > 1:
                    parts = [p + q for p, q in zip(parts[::2], parts[1::2])]
                t[i][h] = x - parts[0]
        t[b] = factor
    return t


def basis_kernel(scale, block, m_ref, s_ref, k_hbm, q_hbm, c_ref, keys, out, tri, in_sem, out_sem):
    tokens, cols = keys.shape
    rank = s_ref.shape[1]
    steps = tokens // block
    load = pltpu.make_async_copy(k_hbm, keys, in_sem)
    load.start()
    sketch = s_ref[...]
    wide = cols // COLS_OUT
    m = jnp.concatenate(
        [
            jnp.concatenate([m_ref[r * wide + c] for c in range(wide)], axis=1)
            for r in range(rank // ROWS_OUT)
        ],
        axis=0,
    )
    pieces = split3(m)
    gram = jnp.zeros((rank, rank), F32)
    for piece in reversed(pieces):
        gram += dot(piece, sketch, 1, 0)
    tri[...] = jnp.zeros_like(tri)
    tri[:, :rank] = gram
    n, lanes = rank // 8, tri.shape[1] // 128
    t = [
        [tri[8 * i : 8 * i + 8, 128 * h : 128 * h + 128] for h in range(lanes)]
        for i in range(n)
    ]
    t = invert_factor(t)
    sub = lax.broadcasted_iota(jnp.int32, (8, 128), 0)
    lane = lax.broadcasted_iota(jnp.int32, (8, 128), 1)
    for i in range(n):
        for h in range(lanes):
            keep = lane + 128 * h <= sub + 8 * i
            tri[8 * i : 8 * i + 8, 128 * h : 128 * h + 128] = jnp.where(keep, t[i][h], 0.0)
    inverse = tri[:, :rank]
    a, b, c = split3(inverse)
    weights = scale * (dot(sketch, c, 1, 1) + dot(sketch, b, 1, 1) + dot(sketch, a, 1, 1))
    high = weights.astype(BF16)
    low = (weights - high.astype(F32)).astype(BF16)
    c_ref[...] = (
        dot(a, pieces[2], 1, 0) + dot(c, pieces[0], 1, 0) + dot(b, pieces[1], 1, 0)
        + dot(a, pieces[1], 1, 0) + dot(b, pieces[0], 1, 0) + dot(a, pieces[0], 1, 0)
    )
    load.wait()
    for i in range(steps):
        rows = pl.ds(i * block, block)
        x = keys[rows, :]
        out[rows, :] = (dot(x, low, 1, 0) + dot(x, high, 1, 0)).astype(BF16)
        pltpu.make_async_copy(out.at[rows, :], q_hbm.at[rows, :], out_sem.at[i]).start()
    for i in range(steps):
        rows = pl.ds(i * block, block)
        pltpu.make_async_copy(out.at[rows, :], q_hbm.at[rows, :], out_sem.at[i]).wait()


def finish(m, sketch, keys, total_tokens, block=512):
    tokens, cols = keys.shape
    rank = sketch.shape[1]
    vmem = pl.BlockSpec(memory_space=pltpu.VMEM)
    return pl.pallas_call(
        functools.partial(basis_kernel, float(total_tokens) ** 0.5, block),
        out_shape=(
            jax.ShapeDtypeStruct((tokens, rank), BF16),
            jax.ShapeDtypeStruct((rank, cols), F32),
        ),
        in_specs=[vmem, vmem, pl.BlockSpec(memory_space=pl.ANY)],
        out_specs=(pl.BlockSpec(memory_space=pl.ANY), vmem),
        scratch_shapes=[
            pltpu.VMEM((tokens, cols), BF16),
            pltpu.VMEM((tokens, rank), BF16),
            pltpu.VMEM((rank, -(-rank // 128) * 128), F32),
            pltpu.SemaphoreType.DMA,
            pltpu.SemaphoreType.DMA((tokens // block,)),
        ],
        compiler_params=pltpu.CompilerParams(vmem_limit_bytes=32 * MIB),
        name="basis",
    )(m, sketch, keys)


def spread(x, axis):
    n = lax.axis_size(axis)
    return lax.all_to_all(jnp.broadcast_to(x[None], (n,) + x.shape), axis, 0, 0)


def sum_over_seq(m):
    part = lax.all_to_all(m, "inner", 0, 0).sum(0)
    part = spread(part, "outer").sum(0)
    return spread(part, "inner")


def body(keys, sketch):
    total_tokens = keys.shape[0] * lax.axis_size("outer") * lax.axis_size("inner")
    m = sum_over_seq(moments(keys, sketch))
    return finish(m, sketch, keys, total_tokens)


def solution(mesh):
    seq, head = mesh.shape["seq"], mesh.shape["head"]
    devices = mesh.devices.reshape(seq // INNER, INNER, head)
    return jax.shard_map(
        body,
        mesh=Mesh(devices, ("outer", "inner", "head")),
        in_specs=(P(("outer", "inner"), "head"), P()),
        out_specs=(P(("outer", "inner"), "head"), P("head", None)),
        check_vma=False,
    )
```

time: 466 us -> 63.7 us (0.14)
  waiting for transfers between devices: 379 us -> 0 us
  other arithmetic: 49.3 us -> 1.01 us
  blocking collectives: 0 us -> 40.1 us
  Pallas kernels: 0 us -> 15.1 us
  between operations: 15.5 us -> 0.69 us
  matrix products: 14.6 us -> 0 us
    psum x2 -> x0, waiting for transfers between devices: 379 us -> none  [the longest x1 191 us: body(): gram = lax.psum(local_gram, 'seq')]
    another operation x13 -> x0, other arithmetic: 47.7 us -> none  [the longest x7 26.4 us: invert_lower(): lower = jnp.linalg.cholesky(gram)]
    all_to_all x0 -> x3, blocking collectives: none -> 40.1 us  [the longest x2 22.4 us: spread(): return lax.all_to_all(jnp.broadcast_to(x[None], (n,) + x.shape), axis, 0, 0)]
    pallas_call x0 -> x2, Pallas kernels: none -> 15.1 us  [the longest x1 12.1 us: finish(): pl.pallas_call(functools.partial(basis_kernel, float(total_tokens) ** 0.5...]
    dot_general x5 -> x0, matrix products: 11.2 us -> none  [the longest x1 4.49 us: body(): orthonormal = jnp.dot(sampled, inverse.T, precision=lax.Precision.HIGHEST)]
  transfers between devices with their start and end apart: 2 -> 0, of which waited for: 2 -> 0; matrix products, arithmetic and copies ran while one was open for 0% -> 0% of each run, Pallas kernels for 0% -> 0%
where the time goes in v1:
time: 63.7 us; the launch traced here: 63.4 us
  blocking collectives  40.1 us (63%)
  Pallas kernels  15.1 us (24%)
  local copies, waits for them, and re-layouts  6.53 us (10%)
  other arithmetic  1.01 us (2%)
  between operations  0.69 us (1%)
    all_to_all x2, blocking collectives, spread(): return lax.all_to_all(jnp.broadcast_to(x[None], (n,) + x.shape), axis, 0, 0)  22.4 us
    all_to_all x1, blocking collectives, sum_over_seq(): part = lax.all_to_all(m, 'inner', 0, 0).sum(0)  17.7 us
    pallas_call x1, Pallas kernels, finish(): pl.pallas_call(functools.partial(basis_kernel, float(total_tokens) ** 0.5...  12.1 us
    unnamed x7, local copies, waits for them, and re-layouts  4.08 us
    pallas_call x1, Pallas kernels, moments(): pl.pallas_call(moments_kernel, grid=(tokens // block,), out_shape=jax.Sha...  3 us
    pallas_call x1, local copies, waits for them, and re-layouts, finish(): pl.pallas_call(functools.partial(basis_kernel, float(total_tokens) ** 0.5...  2.42 us

profile of v1, /device:TPU:1, one launch (start us, length us, event | category | flops | bytes accessed | tf_op | source)
XLA Modules:
  0.0 63.4 jit_solution(6805174632016571407)
XLA Ops:
  0.6 1.0 %copy.7.s_ref = bf16[512,160]{1,0:T(8,128)(2,1)S(1)} copy(bf16[512,160]{0,1:T(8,128)(2,1)} %param.3) | data formatting | bytes 327680 | tf_op args[1]
  1.7 0.0 copy-start
  1.7 1.9 %copy-done = bf16[3072,512]{1,0:T(8,128)(2,1)S(1)} copy-done((bf16[3072,512]{1,0:T(8,128)(2,1)S(1)}, bf16[3072,512]{1,0:T(8,128)(2,1)}, u32[]{:S(2)}) %copy-start) | copy-done | bytes 3145752
  3.6 0.0 copy-start.1
  3.6 3.0 %moments.1 = f32[16,40,128]{2,1,0:T(8,128)S(1)} custom-call(bf16[3072,512]{1,0:T(8,128)(2,1)S(1)} %copy-done, bf16[512,160]{1,0:T(8,128)(2,1)S(1)} %copy.7.s_ref), custom_call_target="tpu_custom_call" | custom-call | tf_op jit(solution)/shard_map/moments/pallas_call | solution.py:60
  6.6 17.7 %all_to_all.15 = f32[16,40,128]{2,1,0:T(8,128)} all-to-all(f32[16,40,128]{2,1,0:T(8,128)S(1)} %moments.1), channel_id=1, replica_groups=mesh['outer'=4,'inner'=16,'head'=8] {'inner'}, dimensions={0} | all-to-all | bytes 655360 | tf_op jit(solution)/shard_map/all_to_all | solution.py:204
  24.3 1.0 %reduce_sum.18 = f32[40,128]{1,0:T(8,128)S(1)} reduce(f32[16,40,128]{2,1,0:T(8,128)} %all_to_all.15, f32[]{:T(128)} %constant.0.clone.1), dimensions={0}, to_apply=%region_0.0 | reduce | flops 76800 | bytes 348164 | tf_op jit(solution)/shard_map/reduce_sum | solution.py:204
  25.3 9.5 %all_to_all.16 = f32[4,40,128]{2,1,0:T(8,128)S(1)} all-to-all(f32[4,40,128]{2,1,0:T(8,128)S(1)} %broadcast_in_dim.4), channel_id=1, replica_groups=mesh['outer'=4,'inner'=16,'head'=8] {'outer'}, dimensions={0} | all-to-all | bytes 163840 | tf_op jit(solution)/shard_map/all_to_all | solution.py:200
  34.8 12.9 %all_to_all.17.m_ref = f32[16,40,128]{2,1,0:T(8,128)S(1)} all-to-all(f32[16,40,128]{2,1,0:T(8,128)S(1)} %broadcast_in_dim.5), channel_id=1, replica_groups=mesh['outer'=4,'inner'=16,'head'=8] {'inner'}, dimensions={0} | all-to-all | bytes 655360 | tf_op jit(solution)/shard_map/all_to_all | solution.py:200
  47.7 0.0 copy-done.1
  47.8 12.1 %basis.1 = (bf16[3072,160]{1,0:T(8,128)(2,1)S(1)}, f32[160,512]{1,0:T(8,128)}) custom-call(f32[16,40,128]{2,1,0:T(8,128)S(1)} %all_to_all.17.m_ref, bf16[512,160]{1,0:T(8,128)(2,1)S(1)} %copy.7.s_ref, bf16[3072,512]{1,0:T(8,128)(2,1)S(1)} %copy-done.1), custom_call_target="tpu_custom_call" | custom-call | tf_op jit(solution)/shard_map/basis/pallas_call | solution.py:178
  59.8 0.0 copy-start.2
  59.8 1.1 %copy-done.2 = bf16[3072,160]{1,0:T(8,128)(2,1)} copy-done((bf16[3072,160]{1,0:T(8,128)(2,1)}, bf16[3072,160]{1,0:T(8,128)(2,1)S(1)}, u32[]{:S(2)}) %copy-start.2) | copy-done | bytes 983064
  61.0 2.4 %copy.9 = bf16[3072,160]{0,1:T(8,128)(2,1)} copy(bf16[3072,160]{1,0:T(8,128)(2,1)} %copy-done.2) | data formatting | bytes 1966080 | tf_op jit(solution)/shard_map/basis/pallas_call | solution.py:178
  (3 shorter events, 0.0 us)
Async XLA Ops:
  1.7 1.9 %copy-start = (bf16[3072,512]{1,0:T(8,128)(2,1)S(1)}, bf16[3072,512]{1,0:T(8,128)(2,1)}, u32[]{:S(2)}) copy-start(bf16[3072,512]{1,0:T(8,128)(2,1)} %k_hbm.1) | copy-start | bytes 9437188
  3.6 44.2 %copy-start.1 = (bf16[3072,512]{1,0:T(8,128)(2,1)S(1)}, bf16[3072,512]{1,0:T(8,128)(2,1)}, u32[]{:S(2)}) copy-start(bf16[3072,512]{1,0:T(8,128)(2,1)} %k_hbm.1) | copy-start | bytes 9437188
  59.8 1.2 %copy-start.2 = (bf16[3072,160]{1,0:T(8,128)(2,1)}, bf16[3072,160]{1,0:T(8,128)(2,1)S(1)}, u32[]{:S(2)}) copy-start(bf16[3072,160]{1,0:T(8,128)(2,1)S(1)} %get-tuple-element.4) | copy-start | bytes 2949124

commit v2 on v1

--- a/solution.py
+++ b/solution.py
@@ -24,26 +24,33 @@
     return a, b, (rest - b.astype(F32)).astype(BF16)
 
 
-def moments_kernel(k_ref, s_ref, m_ref, acc):
-    step = pl.program_id(0)
-    keys = k_ref[...]
-    part = dot(keys, keys, 0, 0)
-
-    @pl.when(step == 0)
-    def _():
-        acc[...] = part
-
-    @pl.when(step > 0)
-    def _():
-        acc[...] += part
-
-    @pl.when(step == pl.num_programs(0) - 1)
-    def _():
-        sketch = s_ref[...]
-        total = jnp.zeros((sketch.shape[1], acc.shape[1]), F32)
-        for piece in reversed(split3(acc[...])):
-            total += dot(sketch, piece, 0, 0)
-        put_chunks(m_ref, total)
+def moments_kernel(block, k_hbm, st_hbm, m_ref, keys, st_ref, sem, st_sem):
+    tokens, cols = keys.shape
+    half = cols // 2
+    copies = []
+    for i in range(tokens // block):
+        rows = pl.ds(i * block, block)
+        copies.append(pltpu.make_async_copy(k_hbm.at[rows, :], keys.at[rows, :], sem.at[i]))
+        copies[-1].start()
+    st_copy = pltpu.make_async_copy(st_hbm, st_ref, st_sem)
+    st_copy.start()
+    top = jnp.zeros((half, cols), F32)
+    low = jnp.zeros((half, half), F32)
+    for i, copy in enumerate(copies):
+        copy.wait()
+        left = keys[i * block : (i + 1) * block, :half]
+        right = keys[i * block : (i + 1) * block, half:]
+        top += dot(left, keys[i * block : (i + 1) * block, :], 0, 0)
+        low += dot(right, right, 0, 0)
+    st_copy.wait()
+    st = st_ref[...]
+    first, second = st[:, :half], st[:, half:]
+    m_left = jnp.zeros((st.shape[0], half), F32)
+    m_right = jnp.zeros((st.shape[0], half), F32)
+    for upper, lower in zip(reversed(split3(top)), reversed(split3(low))):
+        m_left += dot(first, upper[:, :half], 1, 0) + dot(second, upper[:, half:], 1, 1)
+        m_right += dot(first, upper[:, half:], 1, 0) + dot(second, lower, 1, 0)
+    put_chunks(m_ref, jnp.concatenate([m_left, m_right], axis=1))
 
 
 def put_chunks(ref, m):
@@ -53,23 +60,29 @@
         ref[i] = m[r : r + ROWS_OUT, c : c + COLS_OUT]
 
 
-def moments(keys, sketch, block=1024):
-    tokens, cols = keys.shape
-    rank = sketch.shape[1]
+def in_hbm(x):
+    return pltpu.with_memory_space_constraint(x, pltpu.HBM)
+
+
+def moments(keys, sketch_t, block=768):
+    tokens, cols = keys.shape
+    rank = sketch_t.shape[0]
     chunks = (rank // ROWS_OUT) * (cols // COLS_OUT)
+    vmem = pl.BlockSpec(memory_space=pltpu.VMEM)
     return pl.pallas_call(
-        moments_kernel,
-        grid=(tokens // block,),
+        functools.partial(moments_kernel, block),
         out_shape=jax.ShapeDtypeStruct((chunks, ROWS_OUT, COLS_OUT), F32),
-        in_specs=[
-            pl.BlockSpec((block, cols), lambda i: (i, 0)),
-            pl.BlockSpec((cols, rank), lambda i: (0, 0)),
+        in_specs=[pl.BlockSpec(memory_space=pltpu.HBM)] * 2,
+        out_specs=vmem,
+        scratch_shapes=[
+            pltpu.VMEM((tokens, cols), BF16),
+            pltpu.VMEM((rank, cols), BF16),
+            pltpu.SemaphoreType.DMA((tokens // block,)),
+            pltpu.SemaphoreType.DMA,
         ],
-        out_specs=pl.BlockSpec((chunks, ROWS_OUT, COLS_OUT), lambda i: (0, 0, 0)),
-        scratch_shapes=[pltpu.VMEM((cols, cols), F32)],
         compiler_params=pltpu.CompilerParams(vmem_limit_bytes=24 * MIB),
         name="moments",
-    )(keys, sketch)
+    )(in_hbm(keys), in_hbm(sketch_t))
 
 
 def lanes_of(tile, j):
@@ -118,13 +131,16 @@
     return t
 
 
-def basis_kernel(scale, block, m_ref, s_ref, k_hbm, q_hbm, c_ref, keys, out, tri, in_sem, out_sem):
-    tokens, cols = keys.shape
-    rank = s_ref.shape[1]
+def basis_kernel(
+    scale, block, m_ref, st_hbm, k_hbm, qt_hbm, c_hbm, keys, st_ref, out, coef, tri, in_sem, st_sem, out_sem, c_sem
+):
+    tokens, cols = keys.shape
+    rank = st_ref.shape[0]
     steps = tokens // block
+    st_copy = pltpu.make_async_copy(st_hbm, st_ref, st_sem)
+    st_copy.start()
     load = pltpu.make_async_copy(k_hbm, keys, in_sem)
     load.start()
-    sketch = s_ref[...]
     wide = cols // COLS_OUT
     m = jnp.concatenate(
         [
@@ -134,9 +150,11 @@
         axis=0,
     )
     pieces = split3(m)
+    st_copy.wait()
+    st = st_ref[...]
     gram = jnp.zeros((rank, rank), F32)
     for piece in reversed(pieces):
-        gram += dot(piece, sketch, 1, 0)
+        gram += dot(piece, st, 1, 1)
     tri[...] = jnp.zeros_like(tri)
     tri[:, :rank] = gram
     n, lanes = rank // 8, tri.shape[1] // 128
@@ -151,48 +169,57 @@
         for h in range(lanes):
             keep = lane + 128 * h <= sub + 8 * i
             tri[8 * i : 8 * i + 8, 128 * h : 128 * h + 128] = jnp.where(keep, t[i][h], 0.0)
-    inverse = tri[:, :rank]
-    a, b, c = split3(inverse)
-    weights = scale * (dot(sketch, c, 1, 1) + dot(sketch, b, 1, 1) + dot(sketch, a, 1, 1))
+    a, b, c = split3(tri[:, :rank])
+    weights = scale * (dot(c, st, 1, 0) + dot(b, st, 1, 0) + dot(a, st, 1, 0))
     high = weights.astype(BF16)
     low = (weights - high.astype(F32)).astype(BF16)
-    c_ref[...] = (
+    both = jnp.concatenate([high, low], axis=0)
+    coef[...] = (
         dot(a, pieces[2], 1, 0) + dot(c, pieces[0], 1, 0) + dot(b, pieces[1], 1, 0)
         + dot(a, pieces[1], 1, 0) + dot(b, pieces[0], 1, 0) + dot(a, pieces[0], 1, 0)
     )
+    c_out = pltpu.make_async_copy(coef, c_hbm, c_sem)
+    c_out.start()
     load.wait()
+    copies = []
     for i in range(steps):
         rows = pl.ds(i * block, block)
-        x = keys[rows, :]
-        out[rows, :] = (dot(x, low, 1, 0) + dot(x, high, 1, 0)).astype(BF16)
-        pltpu.make_async_copy(out.at[rows, :], q_hbm.at[rows, :], out_sem.at[i]).start()
-    for i in range(steps):
-        rows = pl.ds(i * block, block)
-        pltpu.make_async_copy(out.at[rows, :], q_hbm.at[rows, :], out_sem.at[i]).wait()
-
-
-def finish(m, sketch, keys, total_tokens, block=512):
-    tokens, cols = keys.shape
-    rank = sketch.shape[1]
+        y = dot(both, keys[rows, :], 1, 1)
+        out[:, rows] = (y[:rank] + y[rank:]).astype(BF16)
+        copies.append(pltpu.make_async_copy(out.at[:, rows], qt_hbm.at[:, rows], out_sem.at[i]))
+        copies[-1].start()
+    c_out.wait()
+    for copy in copies:
+        copy.wait()
+
+
+def finish(m, sketch_t, keys, total_tokens, block=512):
+    tokens, cols = keys.shape
+    rank = sketch_t.shape[0]
     vmem = pl.BlockSpec(memory_space=pltpu.VMEM)
+    hbm = pl.BlockSpec(memory_space=pltpu.HBM)
     return pl.pallas_call(
         functools.partial(basis_kernel, float(total_tokens) ** 0.5, block),
         out_shape=(
-            jax.ShapeDtypeStruct((tokens, rank), BF16),
+            jax.ShapeDtypeStruct((rank, tokens), BF16),
             jax.ShapeDtypeStruct((rank, cols), F32),
         ),
-        in_specs=[vmem, vmem, pl.BlockSpec(memory_space=pl.ANY)],
-        out_specs=(pl.BlockSpec(memory_space=pl.ANY), vmem),
+        in_specs=[vmem, hbm, hbm],
+        out_specs=(hbm, hbm),
         scratch_shapes=[
             pltpu.VMEM((tokens, cols), BF16),
-            pltpu.VMEM((tokens, rank), BF16),
+            pltpu.VMEM((rank, cols), BF16),
+            pltpu.VMEM((rank, tokens), BF16),
+            pltpu.VMEM((rank, cols), F32),
             pltpu.VMEM((rank, -(-rank // 128) * 128), F32),
             pltpu.SemaphoreType.DMA,
+            pltpu.SemaphoreType.DMA,
             pltpu.SemaphoreType.DMA((tokens // block,)),
+            pltpu.SemaphoreType.DMA,
         ],
         compiler_params=pltpu.CompilerParams(vmem_limit_bytes=32 * MIB),
         name="basis",
-    )(m, sketch, keys)
+    )(m, in_hbm(sketch_t), in_hbm(keys))
 
 
 def spread(x, axis):
@@ -208,8 +235,9 @@
 
 def body(keys, sketch):
     total_tokens = keys.shape[0] * lax.axis_size("outer") * lax.axis_size("inner")
-    m = sum_over_seq(moments(keys, sketch))
-    return finish(m, sketch, keys, total_tokens)
+    m = sum_over_seq(moments(keys, sketch.T))
+    basis_t, coefficients = finish(m, sketch.T, keys, total_tokens)
+    return basis_t.T, coefficients
 
 
 def solution(mesh):

time: 63.7 us -> 54.9 us (0.86)
  local copies, waits for them, and re-layouts: 6.53 us -> 0.03 us
  Pallas kernels: 15.1 us -> 14 us
  other arithmetic: 1.01 us -> 0.03 us
    unnamed x7 -> x0, local copies, waits for them, and re-layouts: 4.08 us -> none
    pallas_call x1 -> x0, local copies, waits for them, and re-layouts: 2.42 us -> none  [finish(): pl.pallas_call(functools.partial(basis_kernel, float(total_tokens) ** 0.5...]
    pallas_call x1, Pallas kernels: 12.1 us -> 10 us  [finish(): pl.pallas_call(functools.partial(basis_kernel, float(total_tokens) ** 0.5...]
    pallas_call x1, Pallas kernels: 3 us -> 3.99 us  [moments(): pl.pallas_call(functools.partial(moments_kernel, block), out_shape=jax.Sh...]
    reduce_sum x1, other arithmetic: 1 us -> 0.02 us  [sum_over_seq(): part = lax.all_to_all(m, 'inner', 0, 0).sum(0)]
    all_to_all x1, blocking collectives: 17.7 us -> 17.1 us  [sum_over_seq(): part = lax.all_to_all(m, 'inner', 0, 0).sum(0)]
where the time goes in v2:
time: 54.9 us; the launch traced here: 54.7 us
  blocking collectives  40 us (73%)
  Pallas kernels  14 us (26%)
  between operations  0.66 us (1%)
    all_to_all x2, blocking collectives, spread(): return lax.all_to_all(jnp.broadcast_to(x[None], (n,) + x.shape), axis, 0, 0)  22.9 us
    all_to_all x1, blocking collectives, sum_over_seq(): part = lax.all_to_all(m, 'inner', 0, 0).sum(0)  17.1 us
    pallas_call x1, Pallas kernels, finish(): pl.pallas_call(functools.partial(basis_kernel, float(total_tokens) ** 0.5...  10 us
    pallas_call x1, Pallas kernels, moments(): pl.pallas_call(functools.partial(moments_kernel, block), out_shape=jax.Sh...  3.99 us

profile of v2, /device:TPU:1, one launch (start us, length us, event | category | flops | bytes accessed | tf_op | source)
XLA Modules:
  0.0 54.7 jit_solution(7187764763651398375)
XLA Ops:
  0.6 4.0 %moments.1 = f32[16,40,128]{2,1,0:T(8,128)S(1)} custom-call(bf16[3072,512]{1,0:T(8,128)(2,1)} %k_hbm.3, bf16[160,512]{1,0:T(8,128)(2,1)} %bitcast.2), custom_call_target="tpu_custom_call" | custom-call | tf_op jit(solution)/shard_map/moments/pallas_call | solution.py:72
  4.6 17.1 %all_to_all.15 = f32[16,40,128]{2,1,0:T(8,128)S(1)} all-to-all(f32[16,40,128]{2,1,0:T(8,128)S(1)} %moments.1), channel_id=1, replica_groups=mesh['outer'=4,'inner'=16,'head'=8] {'inner'}, dimensions={0} | all-to-all | bytes 655360 | tf_op jit(solution)/shard_map/all_to_all | solution.py:231
  21.7 10.0 %all_to_all.16 = f32[4,40,128]{2,1,0:T(8,128)S(1)} all-to-all(f32[4,40,128]{2,1,0:T(8,128)S(1)} %broadcast_in_dim.4), channel_id=1, replica_groups=mesh['outer'=4,'inner'=16,'head'=8] {'outer'}, dimensions={0} | all-to-all | bytes 163840 | tf_op jit(solution)/shard_map/all_to_all | solution.py:227
  31.8 12.9 %all_to_all.17.m_ref = f32[16,40,128]{2,1,0:T(8,128)S(1)} all-to-all(f32[16,40,128]{2,1,0:T(8,128)S(1)} %broadcast_in_dim.5), channel_id=1, replica_groups=mesh['outer'=4,'inner'=16,'head'=8] {'inner'}, dimensions={0} | all-to-all | bytes 655360 | tf_op jit(solution)/shard_map/all_to_all | solution.py:227
  44.7 10.0 %basis.1 = (bf16[160,3072]{1,0:T(8,128)(2,1)}, f32[160,512]{1,0:T(8,128)}) custom-call(f32[16,40,128]{2,1,0:T(8,128)S(1)} %all_to_all.17.m_ref, bf16[160,512]{1,0:T(8,128)(2,1)} %bitcast.3, bf16[3072,512]{1,0:T(8,128)(2,1)} %k_hbm.3), custom_call_target="tpu_custom_call" | custom-call | tf_op jit(solution)/shard_map/basis/pallas_call | solution.py:201
  (4 shorter events, 0.1 us)

commit v3 on v2

--- a/solution.py
+++ b/solution.py
@@ -31,13 +31,18 @@
     for i in range(tokens // block):
         rows = pl.ds(i * block, block)
         copies.append(pltpu.make_async_copy(k_hbm.at[rows, :], keys.at[rows, :], sem.at[i]))
-        copies[-1].start()
+    ahead = 2
+    for copy in copies[:ahead]:
+        copy.start()
     st_copy = pltpu.make_async_copy(st_hbm, st_ref, st_sem)
-    st_copy.start()
     top = jnp.zeros((half, cols), F32)
     low = jnp.zeros((half, half), F32)
     for i, copy in enumerate(copies):
         copy.wait()
+        if i + ahead < len(copies):
+            copies[i + ahead].start()
+        if i == 0:
+            st_copy.start()
         left = keys[i * block : (i + 1) * block, :half]
         right = keys[i * block : (i + 1) * block, half:]
         top += dot(left, keys[i * block : (i + 1) * block, :], 0, 0)
@@ -64,7 +69,7 @@
     return pltpu.with_memory_space_constraint(x, pltpu.HBM)
 
 
-def moments(keys, sketch_t, block=768):
+def moments(keys, sketch_t, block=1024):
     tokens, cols = keys.shape
     rank = sketch_t.shape[0]
     chunks = (rank // ROWS_OUT) * (cols // COLS_OUT)
@@ -93,54 +98,90 @@
     return jnp.broadcast_to(tile[s : s + 1, :], (8, 128))
 
 
-def invert_factor(t):
-    n, wide = len(t), len(t[0])
+def invert_factor(t, per=2, panel=4):
+    n, wide, width = len(t), len(t[0]), 8 * per
     sub = lax.broadcasted_iota(jnp.int32, (8, 128), 0)
     lane = lax.broadcasted_iota(jnp.int32, (8, 128), 1)
-    for b in range(n):
-        at, off = b // 16, 8 * (b % 16)
-        cols = [lanes_of(t[b][at], off + s) for s in range(8)]
-        solved, factor = list(t[b]), list(t[b])
-        for s in range(8):
-            here = sub == s
-            pivot = row_of(cols[s], s)
+    for b in range(0, n, per):
+        at, off = 8 * b // 128, 8 * b % 128
+        cols = [[lanes_of(t[b + r][at], off + s) for r in range(per)] for s in range(width)]
+        solved = [list(t[b + r]) for r in range(per)]
+        factor = [list(t[b + r]) for r in range(per)]
+        for s in range(width):
+            p, q = divmod(s, 8)
+            here = sub == q
+            pivot = row_of(cols[s][p], q)
             inv, root = 1.0 / pivot, lax.rsqrt(pivot)
             for h in range(wide):
-                row, old = row_of(solved[h], s), solved[h]
+                row, olds = row_of(solved[p][h], q), [solved[r][h] for r in range(per)]
                 if h == at:
                     row = jnp.where(lane == off + s, 1.0, row)
-                    old = jnp.where(lane == off + s, 0.0, old)
-                factor[h] = jnp.where(here, row * root, factor[h])
+                    olds = [jnp.where(lane == off + s, 0.0, x) for x in olds]
+                factor[p][h] = jnp.where(here, row * root, factor[p][h])
                 row = row * inv
-                solved[h] = jnp.where(here, row, old - cols[s] * row)
-            for k in range(s + 1, 8):
-                val = row_of(cols[k], s) * inv
-                cols[k] = jnp.where(here, val, cols[k] - cols[s] * val)
-        in_block = (lane >= off) & (lane < off + 8)
-        for i in range(b + 1, n):
-            left = [lanes_of(t[i][at], off + s) for s in range(8)]
+                for r in range(per):
+                    x = olds[r] - cols[s][r] * row
+                    solved[r][h] = jnp.where(here, row, x) if r == p else x
+            for k in range(s + 1, width):
+                val = row_of(cols[k][p], q) * inv
+                for r in range(per):
+                    x = cols[k][r] - cols[s][r] * val
+                    cols[k][r] = jnp.where(here, val, x) if r == p else x
+        in_block = (lane >= off) & (lane < off + width)
+        end = min(n, (b // panel + 1) * panel)
+        for i in range(b + per, end):
+            left = [lanes_of(t[i][at], off + s) for s in range(width)]
             for h in range(wide):
-                x = t[i][h]
-                if h == at:
-                    x = jnp.where(in_block, 0.0, x)
-                parts = [left[s] * row_of(solved[h], s) for s in range(8)]
+                x = jnp.where(in_block, 0.0, t[i][h]) if h == at else t[i][h]
+                parts = [left[s] * row_of(solved[s // 8][h], s % 8) for s in range(width)]
                 while len(parts) > 1:
                     parts = [p + q for p, q in zip(parts[::2], parts[1::2])]
                 t[i][h] = x - parts[0]
-        t[b] = factor
+        for r in range(per):
+            t[b + r] = factor[r]
+        if b + per == end and end < n:
+            rows = range(end - panel, end)
+            u = jnp.concatenate(
+                [
+                    jnp.concatenate(
+                        [
+                            jnp.where((lane + 128 * h > sub + 8 * i) & (lane + 128 * h < 8 * end), 0.0, t[i][h])
+                            for h in range(wide)
+                        ],
+                        axis=1,
+                    )
+                    for i in rows
+                ],
+                axis=0,
+            )
+            a1, a2, a3 = split3(u)
+            out = dot(
+                jnp.concatenate([a3, a1, a2, a2, a1, a1], axis=0),
+                jnp.concatenate([a1, a3, a2, a1, a2, a1], axis=0),
+                0,
+                0,
+            )
+            for i in range(end, n):
+                for h in range(wide):
+                    done = (lane + 128 * h >= 8 * (end - panel)) & (lane + 128 * h < 8 * end)
+                    x = jnp.where(done, 0.0, t[i][h])
+                    t[i][h] = x - out[8 * i : 8 * i + 8, 128 * h : 128 * h + 128]
     return t
 
 
 def basis_kernel(
-    scale, block, m_ref, st_hbm, k_hbm, qt_hbm, c_hbm, keys, st_ref, out, coef, tri, in_sem, st_sem, out_sem, c_sem
+    scale, block, m_any, st_any, k_hbm, qt_hbm, c_hbm, m_ref, st_ref, keys, out, coef, tri, first_sem, in_sem, out_sem, c_sem
 ):
     tokens, cols = keys.shape
     rank = st_ref.shape[0]
     steps = tokens // block
-    st_copy = pltpu.make_async_copy(st_hbm, st_ref, st_sem)
+    m_copy = pltpu.make_async_copy(m_any, m_ref, first_sem.at[0])
+    st_copy = pltpu.make_async_copy(st_any, st_ref, first_sem.at[1])
+    m_copy.start()
     st_copy.start()
     load = pltpu.make_async_copy(k_hbm, keys, in_sem)
     load.start()
+    m_copy.wait()
     wide = cols // COLS_OUT
     m = jnp.concatenate(
         [
@@ -196,7 +237,7 @@
 def finish(m, sketch_t, keys, total_tokens, block=512):
     tokens, cols = keys.shape
     rank = sketch_t.shape[0]
-    vmem = pl.BlockSpec(memory_space=pltpu.VMEM)
+    anywhere = pl.BlockSpec(memory_space=pl.ANY)
     hbm = pl.BlockSpec(memory_space=pltpu.HBM)
     return pl.pallas_call(
         functools.partial(basis_kernel, float(total_tokens) ** 0.5, block),
@@ -204,22 +245,23 @@
             jax.ShapeDtypeStruct((rank, tokens), BF16),
             jax.ShapeDtypeStruct((rank, cols), F32),
         ),
-        in_specs=[vmem, hbm, hbm],
+        in_specs=[anywhere, anywhere, hbm],
         out_specs=(hbm, hbm),
         scratch_shapes=[
+            pltpu.VMEM(m.shape, F32),
+            pltpu.VMEM((rank, cols), BF16),
             pltpu.VMEM((tokens, cols), BF16),
-            pltpu.VMEM((rank, cols), BF16),
             pltpu.VMEM((rank, tokens), BF16),
             pltpu.VMEM((rank, cols), F32),
             pltpu.VMEM((rank, -(-rank // 128) * 128), F32),
-            pltpu.SemaphoreType.DMA,
+            pltpu.SemaphoreType.DMA((2,)),
             pltpu.SemaphoreType.DMA,
             pltpu.SemaphoreType.DMA((tokens // block,)),
             pltpu.SemaphoreType.DMA,
         ],
         compiler_params=pltpu.CompilerParams(vmem_limit_bytes=32 * MIB),
         name="basis",
-    )(m, in_hbm(sketch_t), in_hbm(keys))
+    )(m, sketch_t, in_hbm(keys))
 
 
 def spread(x, axis):

time: 54.9 us -> 52.3 us (0.953)
  Pallas kernels: 14 us -> 11.3 us
    pallas_call x1, Pallas kernels: 10 us -> 7.21 us  [finish(): pl.pallas_call(functools.partial(basis_kernel, float(total_tokens) ** 0.5...]
where the time goes in v3:
time: 52.3 us; the launch traced here: 52.1 us
  blocking collectives  40 us (76%)
  Pallas kernels  11.3 us (22%)
  between operations  0.67 us (1%)
    all_to_all x2, blocking collectives, spread(): return lax.all_to_all(jnp.broadcast_to(x[None], (n,) + x.shape), axis, 0, 0)  22.9 us
    all_to_all x1, blocking collectives, sum_over_seq(): part = lax.all_to_all(m, 'inner', 0, 0).sum(0)  17.1 us
    pallas_call x1, Pallas kernels, finish(): pl.pallas_call(functools.partial(basis_kernel, float(total_tokens) ** 0.5...  7.21 us
    pallas_call x1, Pallas kernels, moments(): pl.pallas_call(functools.partial(moments_kernel, block), out_shape=jax.Sh...  4.11 us

profile of v3, /device:TPU:1, one launch (start us, length us, event | category | flops | bytes accessed | tf_op | source)
XLA Modules:
  0.0 52.1 jit_solution(9935816983951718959)
XLA Ops:
  0.6 0.0 copy-start
  0.6 4.1 %moments.1 = f32[16,40,128]{2,1,0:T(8,128)S(1)} custom-call(bf16[3072,512]{1,0:T(8,128)(2,1)} %k_hbm.3, bf16[160,512]{1,0:T(8,128)(2,1)} %bitcast.2), custom_call_target="tpu_custom_call" | custom-call | tf_op jit(solution)/shard_map/moments/pallas_call | solution.py:77
  4.8 17.1 %all_to_all.15 = f32[16,40,128]{2,1,0:T(8,128)S(1)} all-to-all(f32[16,40,128]{2,1,0:T(8,128)S(1)} %moments.1), channel_id=1, replica_groups=mesh['outer'=4,'inner'=16,'head'=8] {'inner'}, dimensions={0} | all-to-all | bytes 655360 | tf_op jit(solution)/shard_map/all_to_all | solution.py:273
  21.9 10.0 %all_to_all.16 = f32[4,40,128]{2,1,0:T(8,128)S(1)} all-to-all(f32[4,40,128]{2,1,0:T(8,128)S(1)} %broadcast_in_dim.4), channel_id=1, replica_groups=mesh['outer'=4,'inner'=16,'head'=8] {'outer'}, dimensions={0} | all-to-all | bytes 163840 | tf_op jit(solution)/shard_map/all_to_all | solution.py:269
  31.9 12.9 %all_to_all.17.m_any = f32[16,40,128]{2,1,0:T(8,128)S(1)} all-to-all(f32[16,40,128]{2,1,0:T(8,128)S(1)} %broadcast_in_dim.5), channel_id=1, replica_groups=mesh['outer'=4,'inner'=16,'head'=8] {'inner'}, dimensions={0} | all-to-all | bytes 655360 | tf_op jit(solution)/shard_map/all_to_all | solution.py:269
  44.8 0.0 copy-done
  44.8 7.2 %basis.1 = (bf16[160,3072]{1,0:T(8,128)(2,1)}, f32[160,512]{1,0:T(8,128)}) custom-call(f32[16,40,128]{2,1,0:T(8,128)S(1)} %all_to_all.17.m_any, bf16[160,512]{1,0:T(8,128)(2,1)S(1)} %bitcast.3, bf16[3072,512]{1,0:T(8,128)(2,1)} %k_hbm.3), custom_call_target="tpu_custom_call" | custom-call | tf_op jit(solution)/shard_map/basis/pallas_call | solution.py:242
  (4 shorter events, 0.1 us)
Async XLA Ops:
  0.6 44.2 %copy-start = (bf16[512,160]{0,1:T(8,128)(2,1)S(1)}, bf16[512,160]{0,1:T(8,128)(2,1)}, u32[]{:S(2)}) copy-start(bf16[512,160]{0,1:T(8,128)(2,1)} %param.3) | copy-start | bytes 491524

commit v4 on v3

--- a/solution.py
+++ b/solution.py
@@ -9,6 +9,7 @@
 
 INNER = 16
 ROWS_OUT, COLS_OUT = 40, 128
+FIRST = 3
 F32, BF16 = jnp.float32, jnp.bfloat16
 MIB = 1 << 20
 
@@ -26,36 +27,24 @@
 
 def moments_kernel(block, k_hbm, st_hbm, m_ref, keys, st_ref, sem, st_sem):
     tokens, cols = keys.shape
-    half = cols // 2
     copies = []
     for i in range(tokens // block):
         rows = pl.ds(i * block, block)
         copies.append(pltpu.make_async_copy(k_hbm.at[rows, :], keys.at[rows, :], sem.at[i]))
-    ahead = 2
-    for copy in copies[:ahead]:
-        copy.start()
+        copies[-1].start()
     st_copy = pltpu.make_async_copy(st_hbm, st_ref, st_sem)
-    top = jnp.zeros((half, cols), F32)
-    low = jnp.zeros((half, half), F32)
+    st_copy.start()
+    both = jnp.zeros((cols, cols), F32)
     for i, copy in enumerate(copies):
         copy.wait()
-        if i + ahead < len(copies):
-            copies[i + ahead].start()
-        if i == 0:
-            st_copy.start()
-        left = keys[i * block : (i + 1) * block, :half]
-        right = keys[i * block : (i + 1) * block, half:]
-        top += dot(left, keys[i * block : (i + 1) * block, :], 0, 0)
-        low += dot(right, right, 0, 0)
+        x = keys[i * block : (i + 1) * block, :]
+        both += dot(x, x, 0, 0)
     st_copy.wait()
     st = st_ref[...]
-    first, second = st[:, :half], st[:, half:]
-    m_left = jnp.zeros((st.shape[0], half), F32)
-    m_right = jnp.zeros((st.shape[0], half), F32)
-    for upper, lower in zip(reversed(split3(top)), reversed(split3(low))):
-        m_left += dot(first, upper[:, :half], 1, 0) + dot(second, upper[:, half:], 1, 1)
-        m_right += dot(first, upper[:, half:], 1, 0) + dot(second, lower, 1, 0)
-    put_chunks(m_ref, jnp.concatenate([m_left, m_right], axis=1))
+    total = jnp.zeros((st.shape[0], cols), F32)
+    for piece in reversed(split3(both)):
+        total += dot(st, piece, 1, 0)
+    put_chunks(m_ref, total)
 
 
 def put_chunks(ref, m):
@@ -98,7 +87,7 @@
     return jnp.broadcast_to(tile[s : s + 1, :], (8, 128))
 
 
-def invert_factor(t, per=2, panel=4):
+def invert_factor(t, per=2, panel=2, beside=lambda block: None):
     n, wide, width = len(t), len(t[0]), 8 * per
     sub = lax.broadcasted_iota(jnp.int32, (8, 128), 0)
     lane = lax.broadcasted_iota(jnp.int32, (8, 128), 1)
@@ -128,8 +117,8 @@
                     x = cols[k][r] - cols[s][r] * val
                     cols[k][r] = jnp.where(here, val, x) if r == p else x
         in_block = (lane >= off) & (lane < off + width)
-        end = min(n, (b // panel + 1) * panel)
-        for i in range(b + per, end):
+        end, far = (b // panel + 1) * panel, min(n, (b // panel + 2) * panel)
+        for i in range(b + per, far):
             left = [lanes_of(t[i][at], off + s) for s in range(width)]
             for h in range(wide):
                 x = jnp.where(in_block, 0.0, t[i][h]) if h == at else t[i][h]
@@ -139,7 +128,8 @@
                 t[i][h] = x - parts[0]
         for r in range(per):
             t[b + r] = factor[r]
-        if b + per == end and end < n:
+        beside(b // per)
+        if b + per == end and far < n:
             rows = range(end - panel, end)
             u = jnp.concatenate(
                 [
@@ -155,22 +145,23 @@
                 axis=0,
             )
             a1, a2, a3 = split3(u)
+            skip = 8 * far // 128 * 128
             out = dot(
-                jnp.concatenate([a3, a1, a2, a2, a1, a1], axis=0),
+                jnp.concatenate([a3, a1, a2, a2, a1, a1], axis=0)[:, skip:],
                 jnp.concatenate([a1, a3, a2, a1, a2, a1], axis=0),
                 0,
                 0,
             )
-            for i in range(end, n):
+            for i in range(far, n):
                 for h in range(wide):
                     done = (lane + 128 * h >= 8 * (end - panel)) & (lane + 128 * h < 8 * end)
                     x = jnp.where(done, 0.0, t[i][h])
-                    t[i][h] = x - out[8 * i : 8 * i + 8, 128 * h : 128 * h + 128]
+                    t[i][h] = x - out[8 * i - skip : 8 * i + 8 - skip, 128 * h : 128 * h + 128]
     return t
 
 
 def basis_kernel(
-    scale, block, m_any, st_any, k_hbm, qt_hbm, c_hbm, m_ref, st_ref, keys, out, coef, tri, first_sem, in_sem, out_sem, c_sem
+    scale, block, m_any, st_any, k_hbm, qt_hbm, c_hbm, m_ref, st_ref, keys, s_high, s_low, out, coef, tri, first_sem, in_sem, out_sem, c_sem
 ):
     tokens, cols = keys.shape
     rank = st_ref.shape[0]
@@ -203,7 +194,19 @@
         [tri[8 * i : 8 * i + 8, 128 * h : 128 * h + 128] for h in range(lanes)]
         for i in range(n)
     ]
-    t = invert_factor(t)
+
+    def sample(step):
+        if step == FIRST:
+            load.wait()
+        i = step - FIRST
+        if 0 <= i < steps:
+            rows = pl.ds(i * block, block)
+            y = dot(st, keys[rows, :], 1, 1)
+            high = y.astype(BF16)
+            s_high[:, rows] = high
+            s_low[:, rows] = (y - high.astype(F32)).astype(BF16)
+
+    t = invert_factor(t, beside=sample)
     sub = lax.broadcasted_iota(jnp.int32, (8, 128), 0)
     lane = lax.broadcasted_iota(jnp.int32, (8, 128), 1)
     for i in range(n):
@@ -211,22 +214,19 @@
             keep = lane + 128 * h <= sub + 8 * i
             tri[8 * i : 8 * i + 8, 128 * h : 128 * h + 128] = jnp.where(keep, t[i][h], 0.0)
     a, b, c = split3(tri[:, :rank])
-    weights = scale * (dot(c, st, 1, 0) + dot(b, st, 1, 0) + dot(a, st, 1, 0))
-    high = weights.astype(BF16)
-    low = (weights - high.astype(F32)).astype(BF16)
+    scaled = scale * tri[:, :rank]
+    high = scaled.astype(BF16)
+    low = (scaled - high.astype(F32)).astype(BF16)
     both = jnp.concatenate([high, low], axis=0)
-    coef[...] = (
-        dot(a, pieces[2], 1, 0) + dot(c, pieces[0], 1, 0) + dot(b, pieces[1], 1, 0)
-        + dot(a, pieces[1], 1, 0) + dot(b, pieces[0], 1, 0) + dot(a, pieces[0], 1, 0)
-    )
+    coef[...] = dot(a, pieces[1], 1, 0) + dot(b, pieces[0], 1, 0) + dot(a, pieces[0], 1, 0)
     c_out = pltpu.make_async_copy(coef, c_hbm, c_sem)
     c_out.start()
-    load.wait()
     copies = []
     for i in range(steps):
         rows = pl.ds(i * block, block)
-        y = dot(both, keys[rows, :], 1, 1)
-        out[:, rows] = (y[:rank] + y[rank:]).astype(BF16)
+        y = dot(both, s_high[:, rows], 1, 0)
+        y = y[:rank] + (y[rank:] + dot(high, s_low[:, rows], 1, 0))
+        out[:, rows] = y.astype(BF16)
         copies.append(pltpu.make_async_copy(out.at[:, rows], qt_hbm.at[:, rows], out_sem.at[i]))
         copies[-1].start()
     c_out.wait()
@@ -252,6 +252,8 @@
             pltpu.VMEM((rank, cols), BF16),
             pltpu.VMEM((tokens, cols), BF16),
             pltpu.VMEM((rank, tokens), BF16),
+            pltpu.VMEM((rank, tokens), BF16),
+            pltpu.VMEM((rank, tokens), BF16),
             pltpu.VMEM((rank, cols), F32),
             pltpu.VMEM((rank, -(-rank // 128) * 128), F32),
             pltpu.SemaphoreType.DMA((2,)),

time: 52.3 us -> 51.3 us (0.981)
  Pallas kernels: 11.3 us -> 10.4 us
    pallas_call x1, Pallas kernels: 7.21 us -> 6.35 us  [finish(): pl.pallas_call(functools.partial(basis_kernel, float(total_tokens) ** 0.5...]
where the time goes in v4:
time: 51.3 us; the launch traced here: 51.1 us
  blocking collectives  40 us (78%)
  Pallas kernels  10.4 us (20%)
  between operations  0.67 us (1%)
    all_to_all x2, blocking collectives, spread(): return lax.all_to_all(jnp.broadcast_to(x[None], (n,) + x.shape), axis, 0, 0)  22.9 us
    all_to_all x1, blocking collectives, sum_over_seq(): part = lax.all_to_all(m, 'inner', 0, 0).sum(0)  17.1 us
    pallas_call x1, Pallas kernels, finish(): pl.pallas_call(functools.partial(basis_kernel, float(total_tokens) ** 0.5...  6.35 us
    pallas_call x1, Pallas kernels, moments(): pl.pallas_call(functools.partial(moments_kernel, block), out_shape=jax.Sh...  4.01 us

profile of v4, /device:TPU:1, one launch (start us, length us, event | category | flops | bytes accessed | tf_op | source)
XLA Modules:
  0.0 51.1 jit_solution(8360541007728692448)
XLA Ops:
  0.6 0.0 copy-start
  0.6 4.0 %moments.1 = f32[16,40,128]{2,1,0:T(8,128)S(1)} custom-call(bf16[3072,512]{1,0:T(8,128)(2,1)} %k_hbm.3, bf16[160,512]{1,0:T(8,128)(2,1)} %bitcast.2), custom_call_target="tpu_custom_call" | custom-call | tf_op jit(solution)/shard_map/moments/pallas_call | solution.py:66
  4.7 17.1 %all_to_all.15 = f32[16,40,128]{2,1,0:T(8,128)S(1)} all-to-all(f32[16,40,128]{2,1,0:T(8,128)S(1)} %moments.1), channel_id=1, replica_groups=mesh['outer'=4,'inner'=16,'head'=8] {'inner'}, dimensions={0} | all-to-all | bytes 655360 | tf_op jit(solution)/shard_map/all_to_all | solution.py:275
  21.8 10.0 %all_to_all.16 = f32[4,40,128]{2,1,0:T(8,128)S(1)} all-to-all(f32[4,40,128]{2,1,0:T(8,128)S(1)} %broadcast_in_dim.4), channel_id=1, replica_groups=mesh['outer'=4,'inner'=16,'head'=8] {'outer'}, dimensions={0} | all-to-all | bytes 163840 | tf_op jit(solution)/shard_map/all_to_all | solution.py:271
  31.8 12.9 %all_to_all.17.m_any = f32[16,40,128]{2,1,0:T(8,128)S(1)} all-to-all(f32[16,40,128]{2,1,0:T(8,128)S(1)} %broadcast_in_dim.5), channel_id=1, replica_groups=mesh['outer'=4,'inner'=16,'head'=8] {'inner'}, dimensions={0} | all-to-all | bytes 655360 | tf_op jit(solution)/shard_map/all_to_all | solution.py:271
  44.7 0.0 copy-done
  44.7 6.3 %basis.1 = (bf16[160,3072]{1,0:T(8,128)(2,1)}, f32[160,512]{1,0:T(8,128)}) custom-call(f32[16,40,128]{2,1,0:T(8,128)S(1)} %all_to_all.17.m_any, bf16[160,512]{1,0:T(8,128)(2,1)S(1)} %bitcast.3, bf16[3072,512]{1,0:T(8,128)(2,1)} %k_hbm.3), custom_call_target="tpu_custom_call" | custom-call | tf_op jit(solution)/shard_map/basis/pallas_call | solution.py:242
  (4 shorter events, 0.1 us)
Async XLA Ops:
  0.6 44.1 %copy-start = (bf16[512,160]{0,1:T(8,128)(2,1)S(1)}, bf16[512,160]{0,1:T(8,128)(2,1)}, u32[]{:S(2)}) copy-start(bf16[512,160]{0,1:T(8,128)(2,1)} %param.3) | copy-start | bytes 491524

commit v5 on v4

--- a/solution.py
+++ b/solution.py
@@ -9,6 +9,7 @@
 
 INNER = 16
 ROWS_OUT, COLS_OUT = 40, 128
+AHEAD = 1
 FIRST = 3
 F32, BF16 = jnp.float32, jnp.bfloat16
 MIB = 1 << 20
@@ -27,6 +28,7 @@
 
 def moments_kernel(block, k_hbm, st_hbm, m_ref, keys, st_ref, sem, st_sem):
     tokens, cols = keys.shape
+    h = cols // 2
     copies = []
     for i in range(tokens // block):
         rows = pl.ds(i * block, block)
@@ -34,17 +36,25 @@
         copies[-1].start()
     st_copy = pltpu.make_async_copy(st_hbm, st_ref, st_sem)
     st_copy.start()
-    both = jnp.zeros((cols, cols), F32)
+    top = jnp.zeros((h, cols), F32)
+    low = jnp.zeros((h, h), F32)
     for i, copy in enumerate(copies):
         copy.wait()
         x = keys[i * block : (i + 1) * block, :]
-        both += dot(x, x, 0, 0)
+        r = x[:, h:]
+        top += dot(x[:, :h], x, 0, 0)
+        low += jnp.concatenate([dot(r[:, : h // 2], r, 0, 0), dot(r[:, h // 2 :], r, 0, 0)], axis=0)
     st_copy.wait()
     st = st_ref[...]
-    total = jnp.zeros((st.shape[0], cols), F32)
-    for piece in reversed(split3(both)):
-        total += dot(st, piece, 1, 0)
-    put_chunks(m_ref, total)
+    tops, lows = split3(top)[::-1], split3(low)[::-1]
+    first = jnp.concatenate([st[:, :h]] * 3, axis=1)
+    second = jnp.concatenate([st[:, h:]] * 3, axis=1)
+    corner = jnp.concatenate([x[:, :h] for x in tops], axis=0)
+    upper = jnp.concatenate([x[:, h:] for x in tops], axis=0)
+    lower_t = jnp.concatenate([x[:, h:] for x in tops], axis=1)
+    left = dot(first, corner, 1, 0) + dot(second, lower_t, 1, 1)
+    right = dot(first, upper, 1, 0) + dot(second, jnp.concatenate(lows, axis=0), 1, 0)
+    put_chunks(m_ref, jnp.concatenate([left, right], axis=1))
 
 
 def put_chunks(ref, m):
@@ -58,7 +68,7 @@
     return pltpu.with_memory_space_constraint(x, pltpu.HBM)
 
 
-def moments(keys, sketch_t, block=1024):
+def moments(keys, sketch_t, block=768):
     tokens, cols = keys.shape
     rank = sketch_t.shape[0]
     chunks = (rank // ROWS_OUT) * (cols // COLS_OUT)
@@ -87,7 +97,7 @@
     return jnp.broadcast_to(tile[s : s + 1, :], (8, 128))
 
 
-def invert_factor(t, per=2, panel=2, beside=lambda block: None):
+def invert_factor(t, per=2, panel=2, beside=lambda block, t: None):
     n, wide, width = len(t), len(t[0]), 8 * per
     sub = lax.broadcasted_iota(jnp.int32, (8, 128), 0)
     lane = lax.broadcasted_iota(jnp.int32, (8, 128), 1)
@@ -128,7 +138,7 @@
                 t[i][h] = x - parts[0]
         for r in range(per):
             t[b + r] = factor[r]
-        beside(b // per)
+        beside(b // per, t)
         if b + per == end and far < n:
             rows = range(end - panel, end)
             u = jnp.concatenate(
@@ -161,7 +171,7 @@
 
 
 def basis_kernel(
-    scale, block, m_any, st_any, k_hbm, qt_hbm, c_hbm, m_ref, st_ref, keys, s_high, s_low, out, coef, tri, first_sem, in_sem, out_sem, c_sem
+    scale, block, m_any, st_any, k_hbm, qt_hbm, c_hbm, m_ref, st_ref, keys, s_high, s_low, out, coef, tri, first_sem, in_sem, out_sem
 ):
     tokens, cols = keys.shape
     rank = st_ref.shape[0]
@@ -195,46 +205,75 @@
         for i in range(n)
     ]
 
-    def sample(step):
+    def halves(x):
+        high = x.astype(BF16)
+        return high, (x - high.astype(F32)).astype(BF16)
+
+    def lower(i, h):
+        sub = lax.broadcasted_iota(jnp.int32, (8, 128), 0)
+        lane = lax.broadcasted_iota(jnp.int32, (8, 128), 1)
+        return jnp.where(lane + 128 * h <= sub + 8 * i, t[i][h], 0.0)
+
+    copies = []
+
+    def send(first, last, rows):
+        piece = (pl.ds(first, last - first), rows)
+        copies.append(pltpu.make_async_copy(out.at[piece], qt_hbm.at[piece], out_sem.at[len(copies)]))
+        copies[-1].start()
+
+    def basis_rows(first, last, x, chunk):
+        depth, count = x.shape[1], last - first
+        high, low = halves(scale * x)
+        rows = pl.ds(chunk * block, block)
+        y = dot(jnp.concatenate([high, low], axis=0), s_high[:depth, rows], 1, 0)
+        y = y[:count] + (y[count:] + dot(high, s_low[:depth, rows], 1, 0))
+        out[first:last, rows] = y.astype(BF16)
+        send(first, last, rows)
+
+    def coefficient_rows(first, last, x):
+        depth = x.shape[1]
+        high, low = halves(x)
+        p = [piece[:depth] for piece in pieces[:2]]
+        coef[first:last, :] = dot(high, p[1], 1, 0) + dot(low, p[0], 1, 0) + dot(high, p[0], 1, 0)
+        piece = (pl.ds(first, last - first), slice(None))
+        copies.append(pltpu.make_async_copy(coef.at[piece], c_hbm.at[piece], out_sem.at[len(copies)]))
+        copies[-1].start()
+
+    early = rank // 128 * 128
+    ready = early // 16 - 1
+
+    def beside(step, t):
         if step == FIRST:
             load.wait()
         i = step - FIRST
         if 0 <= i < steps:
             rows = pl.ds(i * block, block)
             y = dot(st, keys[rows, :], 1, 1)
-            high = y.astype(BF16)
-            s_high[:, rows] = high
-            s_low[:, rows] = (y - high.astype(F32)).astype(BF16)
-
-    t = invert_factor(t, beside=sample)
-    sub = lax.broadcasted_iota(jnp.int32, (8, 128), 0)
-    lane = lax.broadcasted_iota(jnp.int32, (8, 128), 1)
-    for i in range(n):
+            s_high[:, rows], s_low[:, rows] = halves(y)
+        if step >= ready:
+            x = jnp.concatenate(
+                [jnp.concatenate([lower(i, h) for h in range(early // 128)], axis=1) for i in range(early // 8)],
+                axis=0,
+            )
+            for chunk in range(steps):
+                if (chunk < AHEAD) == (step == ready) and step <= ready + 1:
+                    basis_rows(0, early, x, chunk)
+            if step == ready + 1:
+                coefficient_rows(0, early, x)
+
+    t = invert_factor(t, beside=beside)
+    for i in range(early // 8, n):
         for h in range(lanes):
-            keep = lane + 128 * h <= sub + 8 * i
-            tri[8 * i : 8 * i + 8, 128 * h : 128 * h + 128] = jnp.where(keep, t[i][h], 0.0)
-    a, b, c = split3(tri[:, :rank])
-    scaled = scale * tri[:, :rank]
-    high = scaled.astype(BF16)
-    low = (scaled - high.astype(F32)).astype(BF16)
-    both = jnp.concatenate([high, low], axis=0)
-    coef[...] = dot(a, pieces[1], 1, 0) + dot(b, pieces[0], 1, 0) + dot(a, pieces[0], 1, 0)
-    c_out = pltpu.make_async_copy(coef, c_hbm, c_sem)
-    c_out.start()
-    copies = []
-    for i in range(steps):
-        rows = pl.ds(i * block, block)
-        y = dot(both, s_high[:, rows], 1, 0)
-        y = y[:rank] + (y[rank:] + dot(high, s_low[:, rows], 1, 0))
-        out[:, rows] = y.astype(BF16)
-        copies.append(pltpu.make_async_copy(out.at[:, rows], qt_hbm.at[:, rows], out_sem.at[i]))
-        copies[-1].start()
-    c_out.wait()
+            tri[8 * i : 8 * i + 8, 128 * h : 128 * h + 128] = lower(i, h)
+    x = tri[early:, :rank]
+    coefficient_rows(early, rank, x)
+    for chunk in range(steps):
+        basis_rows(early, rank, x, chunk)
     for copy in copies:
         copy.wait()
 
 
-def finish(m, sketch_t, keys, total_tokens, block=512):
+def finish(m, sketch_t, keys, total_tokens, block=1024):
     tokens, cols = keys.shape
     rank = sketch_t.shape[0]
     anywhere = pl.BlockSpec(memory_space=pl.ANY)
@@ -258,8 +297,7 @@
             pltpu.VMEM((rank, -(-rank // 128) * 128), F32),
             pltpu.SemaphoreType.DMA((2,)),
             pltpu.SemaphoreType.DMA,
-            pltpu.SemaphoreType.DMA((tokens // block,)),
-            pltpu.SemaphoreType.DMA,
+            pltpu.SemaphoreType.DMA((2 * (tokens // block) + 2,)),
         ],
         compiler_params=pltpu.CompilerParams(vmem_limit_bytes=32 * MIB),
         name="basis",

time: 51.3 us -> 50.4 us (0.982)
  Pallas kernels: 10.4 us -> 9.45 us
    pallas_call x1, Pallas kernels: 4.01 us -> 3.45 us  [moments(): pl.pallas_call(functools.partial(moments_kernel, block), out_shape=jax.Sh...]
where the time goes in v5:
time: 50.4 us; the launch traced here: 50.2 us
  blocking collectives  40 us (79%)
  Pallas kernels  9.45 us (19%)
  between operations  0.67 us (1%)
    all_to_all x2, blocking collectives, spread(): return lax.all_to_all(jnp.broadcast_to(x[None], (n,) + x.shape), axis, 0, 0)  22.9 us
    all_to_all x1, blocking collectives, sum_over_seq(): part = lax.all_to_all(m, 'inner', 0, 0).sum(0)  17.1 us
    pallas_call x1, Pallas kernels, finish(): pl.pallas_call(functools.partial(basis_kernel, float(total_tokens) ** 0.5...  6 us
    pallas_call x1, Pallas kernels, moments(): pl.pallas_call(functools.partial(moments_kernel, block), out_shape=jax.Sh...  3.45 us

profile of v5, /device:TPU:1, one launch (start us, length us, event | category | flops | bytes accessed | tf_op | source)
XLA Modules:
  0.0 50.2 jit_solution(13936026531681498623)
XLA Ops:
  0.6 0.0 copy-start
  0.6 3.4 %moments.1 = f32[16,40,128]{2,1,0:T(8,128)S(1)} custom-call(bf16[3072,512]{1,0:T(8,128)(2,1)} %k_hbm.3, bf16[160,512]{1,0:T(8,128)(2,1)} %bitcast.2), custom_call_target="tpu_custom_call" | custom-call | tf_op jit(solution)/shard_map/moments/pallas_call | solution.py:76
  4.1 17.1 %all_to_all.15 = f32[16,40,128]{2,1,0:T(8,128)S(1)} all-to-all(f32[16,40,128]{2,1,0:T(8,128)S(1)} %moments.1), channel_id=1, replica_groups=mesh['outer'=4,'inner'=16,'head'=8] {'inner'}, dimensions={0} | all-to-all | bytes 655360 | tf_op jit(solution)/shard_map/all_to_all | solution.py:313
  21.2 10.0 %all_to_all.16 = f32[4,40,128]{2,1,0:T(8,128)S(1)} all-to-all(f32[4,40,128]{2,1,0:T(8,128)S(1)} %broadcast_in_dim.4), channel_id=1, replica_groups=mesh['outer'=4,'inner'=16,'head'=8] {'outer'}, dimensions={0} | all-to-all | bytes 163840 | tf_op jit(solution)/shard_map/all_to_all | solution.py:309
  31.3 12.9 %all_to_all.17.m_any = f32[16,40,128]{2,1,0:T(8,128)S(1)} all-to-all(f32[16,40,128]{2,1,0:T(8,128)S(1)} %broadcast_in_dim.5), channel_id=1, replica_groups=mesh['outer'=4,'inner'=16,'head'=8] {'inner'}, dimensions={0} | all-to-all | bytes 655360 | tf_op jit(solution)/shard_map/all_to_all | solution.py:309
  44.2 0.0 copy-done
  44.2 6.0 %basis.1 = (bf16[160,3072]{1,0:T(8,128)(2,1)}, f32[160,512]{1,0:T(8,128)}) custom-call(f32[16,40,128]{2,1,0:T(8,128)S(1)} %all_to_all.17.m_any, bf16[160,512]{1,0:T(8,128)(2,1)S(1)} %bitcast.3, bf16[3072,512]{1,0:T(8,128)(2,1)} %k_hbm.3), custom_call_target="tpu_custom_call" | custom-call | tf_op jit(solution)/shard_map/basis/pallas_call | solution.py:281
  (4 shorter events, 0.1 us)
Async XLA Ops:
  0.6 43.6 %copy-start = (bf16[512,160]{0,1:T(8,128)(2,1)S(1)}, bf16[512,160]{0,1:T(8,128)(2,1)}, u32[]{:S(2)}) copy-start(bf16[512,160]{0,1:T(8,128)(2,1)} %param.3) | copy-start | bytes 491524

commit v6 on v5

--- a/solution.py
+++ b/solution.py
@@ -9,7 +9,7 @@
 
 INNER = 16
 ROWS_OUT, COLS_OUT = 40, 128
-AHEAD = 1
+AHEAD = 0
 FIRST = 3
 F32, BF16 = jnp.float32, jnp.bfloat16
 MIB = 1 << 20
@@ -101,6 +101,10 @@
     n, wide, width = len(t), len(t[0]), 8 * per
     sub = lax.broadcasted_iota(jnp.int32, (8, 128), 0)
     lane = lax.broadcasted_iota(jnp.int32, (8, 128), 1)
+
+    def above(b, p):
+        return p if b + per == n else 0
+
     for b in range(0, n, per):
         at, off = 8 * b // 128, 8 * b % 128
         cols = [[lanes_of(t[b + r][at], off + s) for r in range(per)] for s in range(width)]
@@ -118,12 +122,12 @@
                     olds = [jnp.where(lane == off + s, 0.0, x) for x in olds]
                 factor[p][h] = jnp.where(here, row * root, factor[p][h])
                 row = row * inv
-                for r in range(per):
+                for r in range(above(b, p), per):
                     x = olds[r] - cols[s][r] * row
                     solved[r][h] = jnp.where(here, row, x) if r == p else x
             for k in range(s + 1, width):
                 val = row_of(cols[k][p], q) * inv
-                for r in range(per):
+                for r in range(above(b, p), per):
                     x = cols[k][r] - cols[s][r] * val
                     cols[k][r] = jnp.where(here, val, x) if r == p else x
         in_block = (lane >= off) & (lane < off + width)
@@ -171,18 +175,15 @@
 
 
 def basis_kernel(
-    scale, block, m_any, st_any, k_hbm, qt_hbm, c_hbm, m_ref, st_ref, keys, s_high, s_low, out, coef, tri, first_sem, in_sem, out_sem
+    scale, block, m_ref, st_any, k_hbm, qt_hbm, c_hbm, st_ref, keys, s_high, s_low, out, coef, tri, first_sem, in_sem, out_sem
 ):
     tokens, cols = keys.shape
     rank = st_ref.shape[0]
     steps = tokens // block
-    m_copy = pltpu.make_async_copy(m_any, m_ref, first_sem.at[0])
-    st_copy = pltpu.make_async_copy(st_any, st_ref, first_sem.at[1])
-    m_copy.start()
+    st_copy = pltpu.make_async_copy(st_any, st_ref, first_sem)
     st_copy.start()
     load = pltpu.make_async_copy(k_hbm, keys, in_sem)
     load.start()
-    m_copy.wait()
     wide = cols // COLS_OUT
     m = jnp.concatenate(
         [
@@ -194,9 +195,8 @@
     pieces = split3(m)
     st_copy.wait()
     st = st_ref[...]
-    gram = jnp.zeros((rank, rank), F32)
-    for piece in reversed(pieces):
-        gram += dot(piece, st, 1, 1)
+    three = dot(jnp.concatenate(pieces, axis=0), st, 1, 1)
+    gram = (three[2 * rank :] + three[rank : 2 * rank]) + three[:rank]
     tri[...] = jnp.zeros_like(tri)
     tri[:, :rank] = gram
     n, lanes = rank // 8, tri.shape[1] // 128
@@ -284,10 +284,9 @@
             jax.ShapeDtypeStruct((rank, tokens), BF16),
             jax.ShapeDtypeStruct((rank, cols), F32),
         ),
-        in_specs=[anywhere, anywhere, hbm],
+        in_specs=[pl.BlockSpec(memory_space=pltpu.VMEM), anywhere, hbm],
         out_specs=(hbm, hbm),
         scratch_shapes=[
-            pltpu.VMEM(m.shape, F32),
             pltpu.VMEM((rank, cols), BF16),
             pltpu.VMEM((tokens, cols), BF16),
             pltpu.VMEM((rank, tokens), BF16),
@@ -295,7 +294,7 @@
             pltpu.VMEM((rank, tokens), BF16),
             pltpu.VMEM((rank, cols), F32),
             pltpu.VMEM((rank, -(-rank // 128) * 128), F32),
-            pltpu.SemaphoreType.DMA((2,)),
+            pltpu.SemaphoreType.DMA,
             pltpu.SemaphoreType.DMA,
             pltpu.SemaphoreType.DMA((2 * (tokens // block) + 2,)),
         ],

time: 50.4 us -> 50.3 us (level)
  no operation moved by 1% of the time
where the time goes in v6:
time: 50.3 us; the launch traced here: 50.1 us
  blocking collectives  40 us (80%)
  Pallas kernels  9.35 us (19%)
  between operations  0.67 us (1%)
    all_to_all x2, blocking collectives, spread(): return lax.all_to_all(jnp.broadcast_to(x[None], (n,) + x.shape), axis, 0, 0)  22.9 us
    all_to_all x1, blocking collectives, sum_over_seq(): part = lax.all_to_all(m, 'inner', 0, 0).sum(0)  17.1 us
    pallas_call x1, Pallas kernels, finish(): pl.pallas_call(functools.partial(basis_kernel, float(total_tokens) ** 0.5...  5.9 us
    pallas_call x1, Pallas kernels, moments(): pl.pallas_call(functools.partial(moments_kernel, block), out_shape=jax.Sh...  3.45 us

profile of v6, /device:TPU:1, one launch (start us, length us, event | category | flops | bytes accessed | tf_op | source)
XLA Modules:
  0.0 50.1 jit_solution(7602409482731377686)
XLA Ops:
  0.6 0.0 copy-start
  0.6 3.4 %moments.1 = f32[16,40,128]{2,1,0:T(8,128)S(1)} custom-call(bf16[3072,512]{1,0:T(8,128)(2,1)} %k_hbm.3, bf16[160,512]{1,0:T(8,128)(2,1)} %bitcast.2), custom_call_target="tpu_custom_call" | custom-call | tf_op jit(solution)/shard_map/moments/pallas_call | solution.py:76
  4.1 17.1 %all_to_all.15 = f32[16,40,128]{2,1,0:T(8,128)S(1)} all-to-all(f32[16,40,128]{2,1,0:T(8,128)S(1)} %moments.1), channel_id=1, replica_groups=mesh['outer'=4,'inner'=16,'head'=8] {'inner'}, dimensions={0} | all-to-all | bytes 655360 | tf_op jit(solution)/shard_map/all_to_all | solution.py:312
  21.2 10.0 %all_to_all.16 = f32[4,40,128]{2,1,0:T(8,128)S(1)} all-to-all(f32[4,40,128]{2,1,0:T(8,128)S(1)} %broadcast_in_dim.4), channel_id=1, replica_groups=mesh['outer'=4,'inner'=16,'head'=8] {'outer'}, dimensions={0} | all-to-all | bytes 163840 | tf_op jit(solution)/shard_map/all_to_all | solution.py:308
  31.3 12.9 %all_to_all.17.m_ref = f32[16,40,128]{2,1,0:T(8,128)S(1)} all-to-all(f32[16,40,128]{2,1,0:T(8,128)S(1)} %broadcast_in_dim.5), channel_id=1, replica_groups=mesh['outer'=4,'inner'=16,'head'=8] {'inner'}, dimensions={0} | all-to-all | bytes 655360 | tf_op jit(solution)/shard_map/all_to_all | solution.py:308
  44.2 0.0 copy-done
  44.2 5.9 %basis.1 = (bf16[160,3072]{1,0:T(8,128)(2,1)}, f32[160,512]{1,0:T(8,128)}) custom-call(f32[16,40,128]{2,1,0:T(8,128)S(1)} %all_to_all.17.m_ref, bf16[160,512]{1,0:T(8,128)(2,1)S(1)} %bitcast.3, bf16[3072,512]{1,0:T(8,128)(2,1)} %k_hbm.3), custom_call_target="tpu_custom_call" | custom-call | tf_op jit(solution)/shard_map/basis/pallas_call | solution.py:281
  (4 shorter events, 0.1 us)
Async XLA Ops:
  0.6 43.6 %copy-start = (bf16[512,160]{0,1:T(8,128)(2,1)S(1)}, bf16[512,160]{0,1:T(8,128)(2,1)}, u32[]{:S(2)}) copy-start(bf16[512,160]{0,1:T(8,128)(2,1)} %param.3) | copy-start | bytes 491524

commit v7 on v6

--- a/solution.py
+++ b/solution.py
@@ -113,8 +113,11 @@
         for s in range(width):
             p, q = divmod(s, 8)
             here = sub == q
-            pivot = row_of(cols[s][p], q)
+            pivot = following if s else row_of(cols[s][p], q)
             inv, root = 1.0 / pivot, lax.rsqrt(pivot)
+            if s + 1 < width:
+                p1, q1 = divmod(s + 1, 8)
+                following = row_of(cols[s + 1][p1], q1) - (row_of(cols[s][p1], q1) * inv) * row_of(cols[s + 1][p], q)
             for h in range(wide):
                 row, olds = row_of(solved[p][h], q), [solved[r][h] for r in range(per)]
                 if h == at:

time: 50.3 us -> 50.3 us (level)
  no operation moved by 1% of the time
where the time goes in v7:
time: 50.3 us; the launch traced here: 50.1 us
  blocking collectives  40 us (80%)
  Pallas kernels  9.34 us (19%)
  between operations  0.67 us (1%)
    all_to_all x2, blocking collectives, spread(): return lax.all_to_all(jnp.broadcast_to(x[None], (n,) + x.shape), axis, 0, 0)  22.9 us
    all_to_all x1, blocking collectives, sum_over_seq(): part = lax.all_to_all(m, 'inner', 0, 0).sum(0)  17.1 us
    pallas_call x1, Pallas kernels, finish(): pl.pallas_call(functools.partial(basis_kernel, float(total_tokens) ** 0.5...  5.89 us
    pallas_call x1, Pallas kernels, moments(): pl.pallas_call(functools.partial(moments_kernel, block), out_shape=jax.Sh...  3.45 us

profile of v7, /device:TPU:1, one launch (start us, length us, event | category | flops | bytes accessed | tf_op | source)
XLA Modules:
  0.0 50.1 jit_solution(11822914789926395640)
XLA Ops:
  0.6 0.0 copy-start
  0.6 3.4 %moments.1 = f32[16,40,128]{2,1,0:T(8,128)S(1)} custom-call(bf16[3072,512]{1,0:T(8,128)(2,1)} %k_hbm.3, bf16[160,512]{1,0:T(8,128)(2,1)} %bitcast.2), custom_call_target="tpu_custom_call" | custom-call | tf_op jit(solution)/shard_map/moments/pallas_call | solution.py:76
  4.1 17.1 %all_to_all.15 = f32[16,40,128]{2,1,0:T(8,128)S(1)} all-to-all(f32[16,40,128]{2,1,0:T(8,128)S(1)} %moments.1), channel_id=1, replica_groups=mesh['outer'=4,'inner'=16,'head'=8] {'inner'}, dimensions={0} | all-to-all | bytes 655360 | tf_op jit(solution)/shard_map/all_to_all | solution.py:315
  21.2 10.0 %all_to_all.16 = f32[4,40,128]{2,1,0:T(8,128)S(1)} all-to-all(f32[4,40,128]{2,1,0:T(8,128)S(1)} %broadcast_in_dim.4), channel_id=1, replica_groups=mesh['outer'=4,'inner'=16,'head'=8] {'outer'}, dimensions={0} | all-to-all | bytes 163840 | tf_op jit(solution)/shard_map/all_to_all | solution.py:311
  31.3 12.9 %all_to_all.17.m_ref = f32[16,40,128]{2,1,0:T(8,128)S(1)} all-to-all(f32[16,40,128]{2,1,0:T(8,128)S(1)} %broadcast_in_dim.5), channel_id=1, replica_groups=mesh['outer'=4,'inner'=16,'head'=8] {'inner'}, dimensions={0} | all-to-all | bytes 655360 | tf_op jit(solution)/shard_map/all_to_all | solution.py:311
  44.2 0.0 copy-done
  44.2 5.9 %basis.1 = (bf16[160,3072]{1,0:T(8,128)(2,1)}, f32[160,512]{1,0:T(8,128)}) custom-call(f32[16,40,128]{2,1,0:T(8,128)S(1)} %all_to_all.17.m_ref, bf16[160,512]{1,0:T(8,128)(2,1)S(1)} %bitcast.3, bf16[3072,512]{1,0:T(8,128)(2,1)} %k_hbm.3), custom_call_target="tpu_custom_call" | custom-call | tf_op jit(solution)/shard_map/basis/pallas_call | solution.py:284
  (4 shorter events, 0.1 us)
Async XLA Ops:
  0.6 43.6 %copy-start = (bf16[512,160]{0,1:T(8,128)(2,1)S(1)}, bf16[512,160]{0,1:T(8,128)(2,1)}, u32[]{:S(2)}) copy-start(bf16[512,160]{0,1:T(8,128)(2,1)} %param.3) | copy-start | bytes 491524
